TPU v7x, 512 devices: a whole 4x8x8 slice. The times are simulated.
512 devices in a mesh: pipe: 4 (over z_lo, core), expert: 32 (over y, z_hi), tensor: 4 (over x).
Axes of the slice: x: 4, y: 8, z: 8 (z_hi: 4, z_lo: 2; z = z_hi * 2 + z_lo), core: 2. Of those that a mesh axis runs over, the one named last changes fastest.
Arguments:
- context: bfloat16 [4, 8192, 2048], P('pipe', 'expert', 'tensor'), may hold values from -6 to 6
- attn_weight: bfloat16 [4, 2048, 2048], P('pipe', 'tensor', 'expert'), may hold values from -0.125 to 0.125
- residual: bfloat16 [4, 8192, 2048], P('pipe', ('expert', 'tensor')), may hold values from -6 to 6
- norm_gain: float32 [4, 2048], P('pipe'), may hold values from 0.25 to 1.75
- centroid: bfloat16 [4, 4, 2048], P('pipe', 'tensor'), may hold values from -0.25 to 0.25
- w_in: bfloat16 [4, 4, 2048, 8192], P('pipe', 'tensor', None, 'expert'), may hold values from -0.125 to 0.125
- w_out: bfloat16 [4, 4, 8192, 2048], P('pipe', 'tensor', 'expert'), may hold values from -0.0625 to 0.0625
- route_order: int32 [4, 128, 64], P('pipe', ('expert', 'tensor')), may hold values from 0 to 63, each once within a row
Outputs:
- handed: bfloat16 [4, 8192, 2048], P('pipe', ('expert', 'tensor'))
Inputs may be any that keep to these rules, and one draw needn't show every extreme that they name: `route_order`: each row of 64 numbers is a permutation of 0 to 63.
All inputs are finite; a program needn't handle non-finite values.
Results may differ from a plain program's by a relative error of at most 0.018.
Values may be sent and summed in bfloat16 or wider, within the bound.
A program may use at most 64 MiB of HBM per device.

v0:
```python
import jax
import jax.numpy as jnp
from jax import lax
from jax.sharding import PartitionSpec as P


def passed_along(block, axis, distance):
    devices = range(lax.axis_size(axis))
    route = [((i - distance) % len(devices), i) for i in devices]
    return lax.ppermute(block, axis, route)


def shards(context, attn_weight, residual, norm_gain, centroid, w_in, w_out, route_order):
    heads_out = context[0]
    out_proj = attn_weight[0]
    row_count = residual.shape[1]
    width = residual.shape[2]
    partial_value = jnp.dot(
        heads_out,
        lax.all_gather(out_proj, "expert", axis=1, tiled=True),
        preferred_element_type=jnp.float32,
    )
    summed_heads = lax.psum(partial_value.astype(jnp.bfloat16), "tensor").astype(jnp.float32)
    attended = lax.dynamic_slice_in_dim(
        summed_heads, lax.axis_index("tensor") * row_count, row_count, 0
    )
    hidden = (residual[0].astype(jnp.float32) + attended).astype(jnp.bfloat16)
    hidden_f = hidden.astype(jnp.float32)
    inverse_rms = lax.rsqrt(jnp.mean(hidden_f * hidden_f, axis=-1, keepdims=True) + 1e-05)
    normed = (hidden_f * inverse_rms * norm_gain[0][None, :]).astype(jnp.bfloat16)
    order_rows = route_order[0, 0]
    group_count = lax.axis_size("tensor")
    per_peer = row_count // group_count
    outgoing = jnp.take(normed, order_rows, axis=0).reshape(group_count, per_peer, width)
    arrived = lax.all_to_all(outgoing, "tensor", split_axis=0, concat_axis=0, tiled=True).reshape(
        row_count, width
    )
    first = w_in[0, 0]
    second = w_out[0, 0]
    gating = centroid[0, 0]
    up_values = jnp.dot(
        lax.all_gather(arrived, "expert", axis=0, tiled=True),
        first,
        preferred_element_type=jnp.float32,
    )
    activated = jax.nn.gelu(up_values, approximate=True).astype(jnp.bfloat16)
    summed = lax.psum_scatter(
        jnp.dot(activated, second, preferred_element_type=jnp.float32).astype(jnp.bfloat16),
        "expert",
        scatter_dimension=0,
        tiled=True,
    ).astype(jnp.float32)
    affinity = jnp.dot(arrived, gating, preferred_element_type=jnp.float32)
    reply = (jax.nn.sigmoid(affinity)[:, None] * summed).astype(jnp.bfloat16)
    returned = lax.all_to_all(
        reply.reshape(group_count, per_peer, width),
        "tensor",
        split_axis=0,
        concat_axis=0,
        tiled=True,
    )
    returned = returned.reshape(row_count, width)
    inverse = jnp.argsort(order_rows)
    expert_out = jnp.take(returned, inverse, axis=0)
    layer_out = (hidden_f + expert_out.astype(jnp.float32)).astype(jnp.bfloat16)
    handed = passed_along(layer_out, "pipe", 1)
    return handed[None]


def solution(mesh):
    return jax.shard_map(
        shards,
        mesh=mesh,
        in_specs=(
            P("pipe", "expert", "tensor"),
            P("pipe", "tensor", "expert"),
            P("pipe", ("expert", "tensor"), None),
            P("pipe", None),
            P("pipe", "tensor", None),
            P("pipe", "tensor", None, "expert"),
            P("pipe", "tensor", "expert", None),
            P("pipe", ("expert", "tensor"), None),
        ),
        out_specs=P("pipe", ("expert", "tensor"), None),
        check_vma=False,
    )
```

profile of v0, /device:TPU:1, one launch (start us, length us, event | category | flops | bytes accessed | tf_op | source)
XLA Modules:
  0.0 595.1 jit_solution(18037080380082336141)
XLA Ops:
  6.5 0.7 all-gather.6.cloned.1.call-update
  7.3 92.7 %all-gather.6.cloned.1.call-done = bf16[1,512,2048]{1,2,0:T(8,128)(2,1)} async-done(((bf16[1,512,64]{1,2,0:T(8,128)(2,1)}), bf16[1,512,2048]{1,2,0:T(8,128)(2,1)}) %all-gather.6.cloned.1.call-update) | async-done | bytes 2097168 | tf_op jit(solution)/shard_map/all_gather | solution.py:20
  100.1 3.4 convolution_convert_fusion.1
  103.5 0.0 all-gather.4.cloned.1.call-start
  103.6 54.1 %all-reduce.2.cloned.1.call-done = bf16[256,2048]{1,0:T(8,128)(2,1)} async-done(((bf16[256,2048]{1,0:T(8,128)(2,1)}), bf16[256,2048]{1,0:T(8,128)(2,1)}) %all-reduce.2.cloned.1.call-update) | async-done | bytes 1048592 | tf_op jit(solution)/shard_map/psum | solution.py:23
  157.8 1.1 fusion.25
  159.0 0.1 fusion.27
  159.1 0.7 gather_fusion
  159.8 0.1 broadcast_select_fusion
  159.9 8.6 %all_to_all.10 = bf16[4,16,2048]{2,1,0:T(8,128)(2,1)} all-to-all(bf16[4,16,2048]{2,1,0:T(8,128)(2,1)S(1)} %bitcast.46), channel_id=1, replica_groups=mesh['pipe'=4,'expert'=32,'tensor'=4] {'tensor'}, dimensions={0} | all-to-all | bytes 524288 | tf_op jit(solution)/shard_map/all_to_all | solution.py:35
  168.6 0.0 reduce-scatter.2.cloned.1.call-start
  168.6 142.9 %all-gather.4.cloned.1.call-done = bf16[2048,2048]{1,0:T(8,128)(2,1)} async-done(((bf16[64,2048]{1,0:T(8,128)(2,1)}), bf16[2048,2048]{1,0:T(8,128)(2,1)}) %all-gather.4.cloned.1.call-update) | async-done | bytes 8388624 | tf_op jit(solution)/shard_map/all_gather | solution.py:42
  311.6 13.0 %convolution_convert_fusion = bf16[2048,2048]{1,0:T(8,128)(2,1)} fusion(bf16[1,1,256,2048]{3,2,1,0:T(8,128)(2,1)S(1)} %copy-done, bf16[2048,2048]{1,0:T(8,128)(2,1)} %all-gather.4.cloned.1.call-done, bf16[1,1,2048,256]{3,2,1,0:T(8,128)(2,1)S(1)} %copy-done.4), kind=kOutput, calls=%fused_computation.2 | convolution fusion | flops 4303880192 | bytes 18874368 | tf_op jit(solution)/shard_map/dot_general | solution.py:48
  324.6 2.0 sort.17
  326.7 0.2 fusion.12
  326.9 237.1 %reduce-scatter.2.cloned.1.call-done = bf16[64,2048]{1,0:T(8,128)(2,1)} async-done(((bf16[2048,2048]{1,0:T(8,128)(2,1)}), bf16[64,2048]{1,0:T(8,128)(2,1)}) %reduce-scatter.2.cloned.1.call-update) | async-done | bytes 262160 | tf_op jit(solution)/shard_map/reduce_scatter | solution.py:47
  564.0 1.8 multiply_convert_fusion
  565.7 4.1 all-to-all-start.1
  569.8 5.5 all-to-all-done.1
  575.4 0.7 gather_fusion.1
  576.1 0.2 fusion.28
  576.3 8.3 %collective-permute-start = (bf16[64,2048]{1,0:T(8,128)(2,1)S(1)}, bf16[64,2048]{1,0:T(8,128)(2,1)S(1)}, u32[]{:S(2)}, u32[]{:S(2)}) collective-permute-start(bf16[64,2048]{1,0:T(8,128)(2,1)S(1)} %fusion.28), channel_id=1, source_target_pairs={{384,0},{0,128},{128,256},{256,384},{385,1},{1,129},{129,257},{257... | collective-permute-start | bytes 786440 | tf_op jit(solution)/shard_map/ppermute | solution.py:10
  584.6 3.3 collective-permute-done
  587.9 0.7 copy.11
  (27 shorter events, 0.2 us)
Async XLA Ops:
  6.5 305.0 %copy-start = (bf16[1,1,256,2048]{3,2,1,0:T(8,128)(2,1)S(1)}, bf16[1,1,256,2048]{3,2,1,0:T(8,128)(2,1)}, u32[]{:S(2)}) copy-start(bf16[1,1,256,2048]{3,2,1,0:T(8,128)(2,1)} %param.16) | copy-start | bytes 3145732
  6.5 93.5 %all-gather.6.cloned.1.call-start = ((), (), s32[]{:S(2)}) async-start(), calls=%async_computation.6 | async-start | bytes 2162688 | tf_op jit(solution)/shard_map/all_gather | solution.py:20
  7.3 96.3 %copy-start.6 = (s32[1,1,64]{2,1,0:T(1,128)S(1)}, s32[1,1,64]{2,1,0:T(1,128)}, u32[]{:S(2)}) copy-start(s32[1,1,64]{2,1,0:T(1,128)} %param.17) | copy-start | bytes 772
  7.3 150.5 %copy-start.2 = (bf16[1,64,2048]{2,1,0:T(8,128)(2,1)S(1)}, bf16[1,64,2048]{2,1,0:T(8,128)(2,1)}, u32[]{:S(2)}) copy-start(bf16[1,64,2048]{2,1,0:T(8,128)(2,1)} %param.12) | copy-start | bytes 786436
  7.3 151.7 %copy-start.3 = (f32[1,2048]{1,0:T(1,128)S(1)}, f32[1,2048]{1,0:T(1,128)}, u32[]{:S(2)}) copy-start(f32[1,2048]{1,0:T(1,128)} %param.13) | copy-start | bytes 24580
  7.3 150.5 %all-reduce.2.cloned.1.call-start = ((), (), s32[]{:S(2)}) async-start(), calls=%async_computation.3 | async-start | bytes 2097152 | tf_op jit(solution)/shard_map/psum | solution.py:23
  103.5 208.1 %all-gather.4.cloned.1.call-start = ((), (), s32[]{:S(2)}) async-start(), calls=%async_computation.4 | async-start | bytes 8650752 | tf_op jit(solution)/shard_map/all_gather | solution.py:42
  158.9 152.6 %copy-start.4 = (bf16[1,1,2048,256]{3,2,1,0:T(8,128)(2,1)S(1)}, bf16[1,1,2048,256]{3,2,1,0:T(8,128)(2,1)}, u32[]{:S(2)}) copy-start(bf16[1,1,2048,256]{3,2,1,0:T(8,128)(2,1)} %param.15) | copy-start | bytes 3145732
  168.6 395.4 %reduce-scatter.2.cloned.1.call-start = ((), (), s32[]{:S(2)}) async-start(), calls=%async_computation.5 | async-start | bytes 8650752 | tf_op jit(solution)/shard_map/reduce_scatter | solution.py:47
  324.6 2.1 copy-start.1
  324.6 2.1 copy-start.5
  565.7 9.6 %all-to-all-start.1 = ((bf16[4,16,2048]{2,1,0:T(8,128)(2,1)}), bf16[4,16,2048]{2,1,0:T(8,128)(2,1)S(1)}, u32[]{:S(2)}, u32[]{:S(2)}) async-start(bf16[4,16,2048]{2,1,0:T(8,128)(2,1)} %bitcast.10), calls=%async_computation.2 | async-start | bytes 524288 | tf_op jit(solution)/shard_map/all_to_all | solution.py:55
  576.3 11.7 %collective-permute-start = (bf16[64,2048]{1,0:T(8,128)(2,1)S(1)}, bf16[64,2048]{1,0:T(8,128)(2,1)S(1)}, u32[]{:S(2)}, u32[]{:S(2)}) collective-permute-start(bf16[64,2048]{1,0:T(8,128)(2,1)S(1)} %fusion.28), channel_id=1, source_target_pairs={{384,0},{0,128},{128,256},{256,384},{385,1},{1,129},{129,257},{257... | collective-permute-start | bytes 786440 | tf_op jit(solution)/shard_map/ppermute | solution.py:10
Sparse Core Ops, SparseCore 0:
  10.5 89.4 all-gather.5
  103.6 54.0 all-reduce.1
  168.7 142.8 all-gather.3
  324.8 239.1 reduce-scatter.1
where the time goes:
time: 596 us; the launch traced here: 595 us
  waiting for transfers between devices  536 us (90%)
  matrix products  16.6 us (3%)
  between operations  13.3 us (2%)
  starting transfers between devices  12.6 us (2%)
  blocking collectives  8.61 us (1%)
    reduce_scatter x1, waiting for transfers between devices, shards(): lax.psum_scatter(jnp.dot(activated, second, preferred_element_type=jnp.fl...  237 us
    all_gather x1, waiting for transfers between devices, shards(): lax.all_gather(arrived, 'expert', axis=0, tiled=True)  143 us
    all_gather x1, waiting for transfers between devices, shards(): lax.all_gather(out_proj, 'expert', axis=1, tiled=True)  92.7 us
    psum x1, waiting for transfers between devices, shards(): lax.psum(partial_value.astype(jnp.bfloat16), 'tensor').astype(jnp.float32)  54.1 us
    dot_general x1, matrix products, shards(): jnp.dot(activated, second, preferred_element_type=jnp.float32)  13 us
  transfers between devices with their start and end apart: 6, of which 6 were waited for; matrix products, arithmetic and copies ran while one was open for 0% of the time, Pallas kernels for 0%

commit v1 on v0

v1 whole, which is shorter than its diff:
```python
import math

import jax
import jax.numpy as jnp
from jax import lax
from jax.experimental import pallas as pl
from jax.experimental.pallas import tpu as pltpu
from jax.sharding import PartitionSpec as P

MESH = pl.DeviceIdType.MESH
F32, BF16 = jnp.float32, jnp.bfloat16
NY, NZ, NX, NP = 8, 4, 4, 4
D, ROWS, HEADS, UNITS = 2048, 64, 512, 256
OFFSETS = (0, 1, -1, 2, -2, 3, -3, 4)
SLOT = {0: 0, 1: 1, -1: 2, 2: 3, -2: 4, 3: 5, -3: 6, 4: 7, -4: 7}
HOPS = 4
DIRS = ((0, 1), (1, -1))
X_BATCHES = ((0, 3), (3, 2), (5, 2), (7, 1))
AG_ORDER = ((0, 1), (2, 3))


def gelu(u):
    inner = math.sqrt(2.0 / math.pi) * (u + 0.044715 * (u * u * u))
    return 0.5 * u * (1.0 + jnp.tanh(inner))


def body(
    ctx, attn, res, gain, cent, w_in, w_out, order, out,
    proj, part, from_x, hidden, outgoing, tokens, w1, w2, act, sums,
    rs_out, rs_in, z_out, z_in, reply, returned, layer, affinity, onehot,
    local_sem, wz_send, wz_recv, pz_send, pz_recv, py_send, py_recv, ax_send, ax_recv,
    dx_send, dx_recv, tz_send, tz_recv, ty_send, ty_recv, ry_send, ry_recv,
    rz_send, rz_recv, bx_send, bx_recv, hp_send, hp_recv,
):
    p, e, t = lax.axis_index("pipe"), lax.axis_index("expert"), lax.axis_index("tensor")
    y, z = e // NZ, e % NZ

    def at_y(step):
        return (p, (y + step + NY) % NY * NZ + z, t)

    def at_z(step):
        return (p, y * NZ + (z + step + NZ) % NZ, t)

    def at_x(step):
        return (p, e, (t + step) % NX)

    pending = []

    def send(src, dst, s_sem, r_sem, to):
        copy = pltpu.make_async_remote_copy(
            src_ref=src, dst_ref=dst, send_sem=s_sem, recv_sem=r_sem,
            device_id=to, device_id_type=MESH,
        )
        copy.start()
        pending.append(copy)
        return copy

    barrier = pltpu.get_barrier_semaphore()
    friends = [at_y(1), at_y(-1), at_z(1), at_z(-1), at_z(2), at_x(1), at_x(2), at_x(3)]
    friends += [((p + 1) % NP, e, t), ((p + NP - 1) % NP, e, t)]
    for friend in friends:
        pl.semaphore_signal(barrier, inc=1, device_id=friend, device_id_type=MESH)

    own_w = (
        pltpu.make_async_copy(w_in, w1.at[:, pl.ds(0, UNITS)], local_sem.at[0]),
        pltpu.make_async_copy(w_out, w2.at[pl.ds(0, UNITS)], local_sem.at[1]),
    )
    for copy in own_w:
        copy.start()

    eye = (
        lax.broadcasted_iota(jnp.int32, (ROWS, ROWS), 0)
        == lax.broadcasted_iota(jnp.int32, (ROWS, ROWS), 1)
    ).astype(BF16)
    columns = lax.dot_general(eye, attn[...], (((1,), (1,)), ((), ())), preferred_element_type=F32)
    proj[0, pl.ds(pl.multiple_of(z * ROWS, ROWS), ROWS), :] = columns.astype(BF16)
    onehot[...] = (lax.broadcasted_iota(jnp.int32, (ROWS, ROWS), 0) == order[...]).astype(BF16)

    pl.semaphore_wait(barrier, len(friends))

    def proj_rows(slot, plane, start=0, count=ROWS):
        return proj.at[slot, pl.ds(pl.multiple_of(plane * ROWS + start, 32), count)]

    planes = (z, (z + NZ - 1) % NZ, (z + 1) % NZ, (z + 2) % NZ)
    pz = [
        send(proj_rows(0, z), proj_rows(0, z), pz_send.at[i], pz_recv.at[i], at_z(step))
        for i, step in enumerate((1, -1, 2))
    ]

    def ring(view, flow, hop, s_sem, r_sem):
        made = []
        for i, step in DIRS:
            part_of = None if hop < HOPS - 1 else i
            src = view(flow, SLOT[-step * hop], part_of)
            dst = view(flow, SLOT[-step * (hop + 1)], part_of)
            made.append(
                send(src, dst, s_sem.at[flow, hop, i], r_sem.at[flow, hop, i], at_y(step))
            )
        return made

    def proj_view(flow, slot, half):
        if half is None:
            return proj_rows(slot, planes[flow])
        return proj_rows(slot, planes[flow], half * 32, 32)

    flying = [ring(proj_view, 0, 0, py_send, py_recv)]

    half = UNITS // 2
    wz = []
    for i, step in DIRS:
        cols = pl.ds(i * half, half)
        there = pl.ds(UNITS + i * half, half)
        wz.append(send(w_in.at[:, cols], w1.at[:, there], wz_send.at[i], wz_recv.at[i], at_z(step)))
    for i, step in DIRS:
        cols = pl.ds(i * half, half)
        there = pl.ds(UNITS + i * half, half)
        wz.append(send(w_out.at[cols], w2.at[there], wz_send.at[2 + i], wz_recv.at[2 + i], at_z(step)))

    for flow in (1, 2, 3):
        pz[flow - 1].wait_recv()
        flying.append(ring(proj_view, flow, 0, py_send, py_recv))

    def project(slot):
        value = lax.dot_general(
            ctx[...], proj[slot], (((1,), (1,)), ((), ())), preferred_element_type=F32
        )
        part[slot] = value.astype(BF16)

    def share(batch):
        first, count = X_BATCHES[batch]
        made = []
        for step in (1, 2, 3):
            rows = pl.ds(pl.multiple_of((t + step) % NX * ROWS, ROWS), ROWS)
            made.append(
                send(
                    part.at[pl.ds(first, count), rows],
                    from_x.at[step - 1, pl.ds(first, count)],
                    ax_send.at[batch, step - 1], ax_recv.at[batch, step - 1], at_x(step),
                )
            )
        return made

    project(0)
    shared = []
    for hop in range(1, HOPS):
        for flow in range(4):
            for copy in flying[flow]:
                copy.wait_recv()
            flying[flow] = ring(proj_view, flow, hop, py_send, py_recv)
        project(2 * hop - 1)
        project(2 * hop)
        shared.append(share(hop - 1))
    for flow in range(4):
        for copy in flying[flow]:
            copy.wait_recv()
    project(7)
    shared.append(share(3))

    squares = jnp.zeros((ROWS, 1), F32)
    for batch, (first, count) in enumerate(X_BATCHES):
        for copy in shared[batch]:
            copy.wait_recv()
        for slot in range(first, first + count):
            mine = part[slot, pl.ds(pl.multiple_of(t * ROWS, ROWS), ROWS), :].astype(F32)
            attended = mine
            for other in range(3):
                attended = attended + from_x[other, slot].astype(F32)
            cols = pl.ds(pl.multiple_of((y + OFFSETS[slot] + NY) % NY * 256, 256), 256)
            value = (res[:, cols].astype(F32) + attended).astype(BF16)
            hidden[:, cols] = value
            wide = value.astype(F32)
            squares = squares + jnp.sum(wide * wide, axis=-1, keepdims=True)
    inverse_rms = lax.rsqrt(squares * (1.0 / D) + 1e-05)
    for c in range(4):
        cols = pl.ds(c * 512, 512)
        normed = (hidden[:, cols].astype(F32) * inverse_rms * gain[:, cols]).astype(BF16)
        picked = lax.dot_general(
            onehot[...], normed, (((0,), (0,)), ((), ())), preferred_element_type=F32
        )
        outgoing[:, cols] = picked.astype(BF16)

    def sixteen(k):
        return pl.ds(pl.multiple_of(k * 16, 16), 16)

    dx = []
    for step in (1, 2, 3):
        dx.append(
            send(
                outgoing.at[sixteen((t + step) % NX)], tokens.at[0, 0, sixteen(t)],
                dx_send.at[step - 1], dx_recv.at[step - 1], at_x(step),
            )
        )
    tokens[0, 0, sixteen(t), :] = outgoing[sixteen(t), :]
    for copy in dx:
        copy.wait_recv()

    def token_view(flow, slot, quarter):
        start, count = flow % 2 * 32, 32
        if quarter is not None:
            start, count = start + quarter * 16, 16
        return tokens.at[flow // 2, slot, pl.ds(start, count)]

    flying = [ring(token_view, flow, 0, ty_send, ty_recv) for flow in (0, 1)]
    tz = []
    for i in range(2):
        rows = pl.ds(i * 32, 32)
        tz.append(
            send(tokens.at[0, 0, rows], tokens.at[1, 0, rows], tz_send.at[i], tz_recv.at[i], at_z(2))
        )

    dots = jnp.zeros((ROWS, 1), F32)
    for c in range(4):
        cols = pl.ds(c * 512, 512)
        dots = dots + jnp.sum(
            tokens[0, 0, :, cols].astype(F32) * cent[:, cols].astype(F32), axis=-1, keepdims=True
        )
    affinity[...] = jnp.broadcast_to(1.0 / (1.0 + jnp.exp(-dots)), (ROWS, 128))

    def pass_on(flow, hop):
        for copy in flying[flow]:
            copy.wait_recv()
        flying[flow] = ring(token_view, flow, hop, ty_send, ty_recv)

    def expert(source, first):
        rows = pl.ds(first * ROWS, 4 * ROWS)
        block = tokens.at[source, pl.ds(first, 4)]

        def up(j, carry):
            cols = pl.ds(pl.multiple_of(j * 256, 256), 256)
            value = jnp.dot(
                block[...].reshape(4 * ROWS, D), w1[:, cols], preferred_element_type=F32
            )
            act[:, cols] = gelu(value).astype(BF16)
            return carry

        lax.fori_loop(0, 2, up, 0)

        def down(j, carry):
            cols = pl.ds(pl.multiple_of(j * 512, 512), 512)
            sums[source, rows, cols] = jnp.dot(act[...], w2[:, cols], preferred_element_type=F32)
            return carry

        lax.fori_loop(0, 4, down, 0)

    for hop in range(1, HOPS):
        for flow in (0, 1):
            pass_on(flow, hop)
    for i in range(2):
        tz[i].wait_recv()
        flying.append(ring(token_view, 2 + i, 0, ty_send, ty_recv))
    for copy in own_w:
        copy.wait()
    for copy in wz:
        copy.wait_recv()
    expert(0, 0)
    for flow in (2, 3):
        pass_on(flow, 1)
    for flow in (0, 1):
        for copy in flying[flow]:
            copy.wait_recv()
    expert(0, 4)
    for flow in (2, 3):
        pass_on(flow, 2)

    rs = {}

    def back(flow, hop):
        source, base = flow // 2, flow % 2 * 32
        for i, step in DIRS:
            slot = SLOT[step * (HOPS - hop)]
            start = slot * ROWS + base
            if hop == 0:
                count = 16
                rs_out[flow, hop, i, pl.ds(0, 16), :] = sums[
                    source, pl.ds(start + i * 16, 16), :
                ].astype(BF16)
            else:
                count = 32
                rs[flow, hop - 1][i].wait_recv()
                for quarter in range(2):
                    rows = pl.ds(quarter * 16, 16)
                    value = sums[source, pl.ds(start + quarter * 16, 16), :]
                    if hop > 1:
                        value = value + rs_in[flow, hop - 1, i, rows, :].astype(F32)
                    elif quarter == i:
                        value = value + rs_in[flow, 0, i, pl.ds(0, 16), :].astype(F32)
                    rs_out[flow, hop, i, rows, :] = value.astype(BF16)
            rs.setdefault((flow, hop), []).append(
                send(
                    rs_out.at[flow, hop, i, pl.ds(0, count)],
                    rs_in.at[flow, hop, i, pl.ds(0, count)],
                    ry_send.at[flow, hop, i], ry_recv.at[flow, hop, i], at_y(step),
                )
            )

    def total(flow):
        source, base = flow // 2, flow % 2 * 32
        for copy in rs[flow, HOPS - 1]:
            copy.wait_recv()
        value = sums[source, pl.ds(base, 32), :]
        for i in range(2):
            value = value + rs_in[flow, HOPS - 1, i].astype(F32)
        return value

    back(0, 0)
    back(1, 0)
    expert(1, 0)
    for flow in (2, 3):
        pass_on(flow, 3)
    back(0, 1)
    back(1, 1)
    for flow in (2, 3):
        for copy in flying[flow]:
            copy.wait_recv()
    expert(1, 4)
    rz = []
    for flow, hop in ((2, 0), (3, 0), (0, 2), (2, 1), (3, 1), (2, 2), (3, 2), (2, 3), (3, 3)):
        back(flow, hop)
    back(1, 2)

    def home(i):
        z_out[i] = total(2 + i).astype(BF16)
        rz.append(send(z_out.at[i], z_in.at[i], rz_send.at[i], rz_recv.at[i], at_z(2)))

    home(0)
    back(0, 3)
    home(1)
    back(1, 3)
    for i in range(2):
        value = total(i)
        rz[i].wait_recv()
        value = value + z_in[i].astype(F32)
        rows = pl.ds(i * 32, 32)
        reply[rows, :] = (affinity[rows, :1] * value).astype(BF16)

    bx = []
    for step in (1, 2, 3):
        bx.append(
            send(
                reply.at[sixteen((t + step) % NX)], returned.at[sixteen(t)],
                bx_send.at[step - 1], bx_recv.at[step - 1], at_x(step),
            )
        )
    returned[sixteen(t), :] = reply[sixteen(t), :]
    for copy in bx:
        copy.wait_recv()
    for c in range(4):
        cols = pl.ds(c * 512, 512)
        placed = jnp.dot(onehot[...], returned[:, cols], preferred_element_type=F32)
        layer[:, cols] = (
            hidden[:, cols].astype(F32) + placed.astype(BF16).astype(F32)
        ).astype(BF16)
    last = send(layer, out, hp_send, hp_recv, ((p + 1) % NP, e, t))
    last.wait_recv()
    for copy in pending:
        copy.wait_send()


def shards(context, attn_weight, residual, norm_gain, centroid, w_in, w_out, route_order):
    vmem, hbm = pl.BlockSpec(memory_space=pltpu.VMEM), pl.BlockSpec(memory_space=pl.ANY)
    dma = pltpu.SemaphoreType.DMA
    flows = (4, HOPS, 2)
    result = pl.pallas_call(
        body,
        out_shape=jax.ShapeDtypeStruct((ROWS, D), BF16),
        in_specs=[vmem, vmem, vmem, vmem, vmem, hbm, hbm, vmem],
        out_specs=hbm,
        scratch_shapes=[
            pltpu.VMEM((NY, 4 * ROWS, HEADS), BF16),
            pltpu.VMEM((NY, 4 * ROWS, 256), BF16),
            pltpu.VMEM((3, NY, ROWS, 256), BF16),
            pltpu.VMEM((ROWS, D), BF16),
            pltpu.VMEM((ROWS, D), BF16),
            pltpu.VMEM((2, NY, ROWS, D), BF16),
            pltpu.VMEM((D, 2 * UNITS), BF16),
            pltpu.VMEM((2 * UNITS, D), BF16),
            pltpu.VMEM((4 * ROWS, 2 * UNITS), BF16),
            pltpu.VMEM((2, NY * ROWS, D), F32),
            pltpu.VMEM((4, HOPS, 2, 32, D), BF16),
            pltpu.VMEM((4, HOPS, 2, 32, D), BF16),
            pltpu.VMEM((2, 32, D), BF16),
            pltpu.VMEM((2, 32, D), BF16),
            pltpu.VMEM((ROWS, D), BF16),
            pltpu.VMEM((ROWS, D), BF16),
            pltpu.VMEM((ROWS, D), BF16),
            pltpu.VMEM((ROWS, 128), F32),
            pltpu.VMEM((ROWS, ROWS), BF16),
            dma((2,)),
            dma((4,)), dma((4,)),
            dma((3,)), dma((3,)),
            dma(flows), dma(flows),
            dma((4, 3)), dma((4, 3)),
            dma((3,)), dma((3,)),
            dma((2,)), dma((2,)),
            dma(flows), dma(flows),
            dma(flows), dma(flows),
            dma((2,)), dma((2,)),
            dma((3,)), dma((3,)),
            dma, dma,
        ],
        compiler_params=pltpu.CompilerParams(
            collective_id=0, has_side_effects=True, vmem_limit_bytes=48 * 2**20
        ),
        cost_estimate=pl.CostEstimate(
            flops=4_800_000_000, bytes_accessed=4_000_000, transcendentals=600_000
        ),
    )(
        context[0], attn_weight[0], residual[0], norm_gain, centroid[0],
        w_in[0, 0], w_out[0, 0], route_order[0],
    )
    return result[None]


def solution(mesh):
    return jax.shard_map(
        shards,
        mesh=mesh,
        in_specs=(
            P("pipe", "expert", "tensor"),
            P("pipe", "tensor", "expert"),
            P("pipe", ("expert", "tensor"), None),
            P("pipe", None),
            P("pipe", "tensor", None),
            P("pipe", "tensor", None, "expert"),
            P("pipe", "tensor", "expert", None),
            P("pipe", ("expert", "tensor"), None),
        ),
        out_specs=P("pipe", ("expert", "tensor"), None),
        check_vma=False,
    )
```

time: 596 us -> 174 us (0.29)
  the two profiles are of different devices: /device:TPU:1 before, /device:TPU:81 now
where the time goes in v1:
time: 174 us
  Pallas kernels  167 us (96%)
  local copies, waits for them, and re-layouts  6.67 us (4%)
    pallas_call x1, Pallas kernels, shards(): pl.pallas_call(body, out_shape=jax.ShapeDtypeStruct((ROWS, D), BF16), in_...  167 us
    unnamed x16, local copies, waits for them, and re-layouts  6.67 us

profile of v1, /device:TPU:81, one launch (start us, length us, event | category | flops | bytes accessed | tf_op | source)
XLA Modules:
  0.0 173.9 jit_solution(13399857852270304693)
XLA Ops:
  0.0 0.0 copy-start.4
  0.0 0.0 copy-start.5
  0.0 1.0 copy.9
  1.0 0.0 copy-start.6
  1.0 0.0 copy-done.4
  1.0 0.0 copy-done.5
  1.0 0.6 copy-done.6
  1.7 0.0 copy-start
  1.7 1.2 copy-done
  2.9 0.0 copy-start.1
  2.9 1.2 copy-done.1
  4.1 0.0 copy-start.2
  4.1 0.9 copy-done.2
  5.1 0.0 copy-start.3
  5.1 0.9 copy-done.3
  6.0 167.2 %shard_map.82 = bf16[64,2048]{1,0:T(8,128)(2,1)S(1)} custom-call(bf16[256,512]{1,0:T(8,128)(2,1)S(1)} %bitcast.12, bf16[512,64]{1,0:T(8,128)(2,1)S(1)} %bitcast.9, bf16[64,2048]{1,0:T(8,128)(2,1)S(1)} %bitcast.13, f32[1,2048]{1,0:T(1,128)S(1)} %copy-done.4, bf16[1,2048]{1,0:T(2,128)(2,1)S(1)} %bitcast.14, bf16[2048,256]{1,0:T(8,128)(2,1)S(1)} %bitcast.10, ...), custom_call_target="tpu_custom_call" | custom-call | flops 4800000000 | bytes 4000000 | tf_op jit(solution)/shard_map/pallas_call | solution.py:363
  173.2 0.7 copy.11
Async XLA Ops:
  0.0 1.0 copy-start.4
  0.0 1.0 copy-start.5
  1.0 0.7 copy-start.6
  1.7 1.2 copy-start
  2.9 1.2 copy-start.1
  4.1 0.9 copy-start.2
  5.1 0.9 copy-start.3

commit v2 on v1

--- a/solution.py
+++ b/solution.py
@@ -11,12 +11,12 @@
 F32, BF16 = jnp.float32, jnp.bfloat16
 NY, NZ, NX, NP = 8, 4, 4, 4
 D, ROWS, HEADS, UNITS = 2048, 64, 512, 256
+WIDE = D // 2
 OFFSETS = (0, 1, -1, 2, -2, 3, -3, 4)
 SLOT = {0: 0, 1: 1, -1: 2, 2: 3, -2: 4, 3: 5, -3: 6, 4: 7, -4: 7}
 HOPS = 4
 DIRS = ((0, 1), (1, -1))
 X_BATCHES = ((0, 3), (3, 2), (5, 2), (7, 1))
-AG_ORDER = ((0, 1), (2, 3))
 
 
 def gelu(u):
@@ -25,8 +25,8 @@
 
 
 def body(
-    ctx, attn, res, gain, cent, w_in, w_out, order, out,
-    proj, part, from_x, hidden, outgoing, tokens, w1, w2, act, sums,
+    ctx_hbm, attn_hbm, res_hbm, gain_hbm, cent_hbm, w_in, w_out, order_hbm, out,
+    ctx, res, gain, cent, order, proj, part, from_x, hidden, outgoing, tokens, w1, w2, act, sums,
     rs_out, rs_in, z_out, z_in, reply, returned, layer, affinity, onehot,
     local_sem, wz_send, wz_recv, pz_send, pz_recv, py_send, py_recv, ax_send, ax_recv,
     dx_send, dx_recv, tz_send, tz_recv, ty_send, ty_recv, ry_send, ry_recv,
@@ -61,25 +61,21 @@
     for friend in friends:
         pl.semaphore_signal(barrier, inc=1, device_id=friend, device_id_type=MESH)
 
-    own_w = (
-        pltpu.make_async_copy(w_in, w1.at[:, pl.ds(0, UNITS)], local_sem.at[0]),
-        pltpu.make_async_copy(w_out, w2.at[pl.ds(0, UNITS)], local_sem.at[1]),
-    )
-    for copy in own_w:
-        copy.start()
-
-    eye = (
-        lax.broadcasted_iota(jnp.int32, (ROWS, ROWS), 0)
-        == lax.broadcasted_iota(jnp.int32, (ROWS, ROWS), 1)
-    ).astype(BF16)
-    columns = lax.dot_general(eye, attn[...], (((1,), (1,)), ((), ())), preferred_element_type=F32)
-    proj[0, pl.ds(pl.multiple_of(z * ROWS, ROWS), ROWS), :] = columns.astype(BF16)
-    onehot[...] = (lax.broadcasted_iota(jnp.int32, (ROWS, ROWS), 0) == order[...]).astype(BF16)
-
-    pl.semaphore_wait(barrier, len(friends))
-
     def proj_rows(slot, plane, start=0, count=ROWS):
         return proj.at[slot, pl.ds(pl.multiple_of(plane * ROWS + start, 32), count)]
+
+    loads = [
+        pltpu.make_async_copy(src, dst, local_sem.at[i])
+        for i, (src, dst) in enumerate((
+            (attn_hbm, proj_rows(0, z)), (ctx_hbm, ctx), (res_hbm, res), (gain_hbm, gain),
+            (cent_hbm, cent), (order_hbm, order),
+            (w_in, w1.at[:, pl.ds(0, UNITS)]), (w_out, w2.at[pl.ds(0, UNITS)]),
+        ))
+    ]
+    for copy in loads:
+        copy.start()
+    loads[0].wait()
+    pl.semaphore_wait(barrier, len(friends))
 
     planes = (z, (z + NZ - 1) % NZ, (z + 1) % NZ, (z + 2) % NZ)
     pz = [
@@ -105,20 +101,21 @@
 
     flying = [ring(proj_view, 0, 0, py_send, py_recv)]
 
-    half = UNITS // 2
-    wz = []
-    for i, step in DIRS:
-        cols = pl.ds(i * half, half)
-        there = pl.ds(UNITS + i * half, half)
-        wz.append(send(w_in.at[:, cols], w1.at[:, there], wz_send.at[i], wz_recv.at[i], at_z(step)))
-    for i, step in DIRS:
-        cols = pl.ds(i * half, half)
-        there = pl.ds(UNITS + i * half, half)
-        wz.append(send(w_out.at[cols], w2.at[there], wz_send.at[2 + i], wz_recv.at[2 + i], at_z(step)))
-
     for flow in (1, 2, 3):
         pz[flow - 1].wait_recv()
         flying.append(ring(proj_view, flow, 0, py_send, py_recv))
+
+    half = UNITS // 2
+
+    def units(i):
+        return pl.ds(i * half, half), pl.ds(UNITS + i * half, half)
+
+    wz_in = []
+    for i, step in DIRS:
+        mine, there = units(i)
+        wz_in.append(
+            send(w_in.at[:, mine], w1.at[:, there], wz_send.at[i], wz_recv.at[i], at_z(step))
+        )
 
     def project(slot):
         value = lax.dot_general(
@@ -140,7 +137,11 @@
             )
         return made
 
+    loads[1].wait()
     project(0)
+    for copy in loads[2:6]:
+        copy.wait()
+    onehot[...] = (lax.broadcasted_iota(jnp.int32, (ROWS, ROWS), 0) == order[...]).astype(BF16)
     shared = []
     for hop in range(1, HOPS):
         for flow in range(4):
@@ -221,26 +222,29 @@
             copy.wait_recv()
         flying[flow] = ring(token_view, flow, hop, ty_send, ty_recv)
 
-    def expert(source, first):
-        rows = pl.ds(first * ROWS, 4 * ROWS)
-        block = tokens.at[source, pl.ds(first, 4)]
-
-        def up(j, carry):
+    def up(source, first):
+        def tile(j, carry):
             cols = pl.ds(pl.multiple_of(j * 256, 256), 256)
             value = jnp.dot(
-                block[...].reshape(4 * ROWS, D), w1[:, cols], preferred_element_type=F32
-            )
-            act[:, cols] = gelu(value).astype(BF16)
+                tokens[source, pl.ds(first, 4)].reshape(4 * ROWS, D), w1[:, cols],
+                preferred_element_type=F32,
+            )
+            act[source, pl.ds(first * ROWS, 4 * ROWS), cols] = gelu(value).astype(BF16)
             return carry
 
-        lax.fori_loop(0, 2, up, 0)
-
-        def down(j, carry):
+        lax.fori_loop(0, 2, tile, 0)
+
+    def down(source, first):
+        rows = pl.ds(first * ROWS, 4 * ROWS)
+
+        def tile(j, carry):
             cols = pl.ds(pl.multiple_of(j * 512, 512), 512)
-            sums[source, rows, cols] = jnp.dot(act[...], w2[:, cols], preferred_element_type=F32)
+            sums[source, rows, cols] = jnp.dot(
+                act[source, rows, :], w2[:, cols], preferred_element_type=F32
+            )
             return carry
 
-        lax.fori_loop(0, 4, down, 0)
+        lax.fori_loop(0, 4, tile, 0)
 
     for hop in range(1, HOPS):
         for flow in (0, 1):
@@ -248,42 +252,52 @@
     for i in range(2):
         tz[i].wait_recv()
         flying.append(ring(token_view, 2 + i, 0, ty_send, ty_recv))
-    for copy in own_w:
+    wz_out = []
+    for i, step in DIRS:
+        mine, there = units(i)
+        wz_out.append(
+            send(w_out.at[mine], w2.at[there], wz_send.at[2 + i], wz_recv.at[2 + i], at_z(step))
+        )
+    for copy in loads[6:]:
         copy.wait()
-    for copy in wz:
+    for copy in wz_in:
         copy.wait_recv()
-    expert(0, 0)
+    up(0, 0)
     for flow in (2, 3):
         pass_on(flow, 1)
     for flow in (0, 1):
         for copy in flying[flow]:
             copy.wait_recv()
-    expert(0, 4)
+    up(0, 4)
     for flow in (2, 3):
         pass_on(flow, 2)
+    up(1, 0)
+    for flow in (2, 3):
+        pass_on(flow, 3)
+    for copy in wz_out:
+        copy.wait_recv()
+    down(0, 4)
 
     rs = {}
 
     def back(flow, hop):
-        source, base = flow // 2, flow % 2 * 32
+        source, cols = flow // 2, pl.ds(flow % 2 * WIDE, WIDE)
         for i, step in DIRS:
-            slot = SLOT[step * (HOPS - hop)]
-            start = slot * ROWS + base
+            start = SLOT[step * (HOPS - hop)] * ROWS
+            count = 32 if hop == 0 else ROWS
             if hop == 0:
-                count = 16
-                rs_out[flow, hop, i, pl.ds(0, 16), :] = sums[
-                    source, pl.ds(start + i * 16, 16), :
+                rs_out[flow, hop, i, pl.ds(0, 32), :] = sums[
+                    source, pl.ds(start + i * 32, 32), cols
                 ].astype(BF16)
             else:
-                count = 32
                 rs[flow, hop - 1][i].wait_recv()
-                for quarter in range(2):
-                    rows = pl.ds(quarter * 16, 16)
-                    value = sums[source, pl.ds(start + quarter * 16, 16), :]
+                for part_of in range(2):
+                    rows = pl.ds(part_of * 32, 32)
+                    value = sums[source, pl.ds(start + part_of * 32, 32), cols]
                     if hop > 1:
                         value = value + rs_in[flow, hop - 1, i, rows, :].astype(F32)
-                    elif quarter == i:
-                        value = value + rs_in[flow, 0, i, pl.ds(0, 16), :].astype(F32)
+                    elif part_of == i:
+                        value = value + rs_in[flow, 0, i, pl.ds(0, 32), :].astype(F32)
                     rs_out[flow, hop, i, rows, :] = value.astype(BF16)
             rs.setdefault((flow, hop), []).append(
                 send(
@@ -294,78 +308,92 @@
             )
 
     def total(flow):
-        source, base = flow // 2, flow % 2 * 32
+        source, cols = flow // 2, pl.ds(flow % 2 * WIDE, WIDE)
         for copy in rs[flow, HOPS - 1]:
             copy.wait_recv()
-        value = sums[source, pl.ds(base, 32), :]
+        value = sums[source, pl.ds(0, ROWS), cols]
         for i in range(2):
             value = value + rs_in[flow, HOPS - 1, i].astype(F32)
         return value
 
+    rz = []
+
+    def home(i):
+        z_out[i] = total(2 + i).astype(BF16)
+        rz.append(send(z_out.at[i], z_in.at[i], rz_send.at[i], rz_recv.at[i], at_z(2)))
+
+    bx = []
+
+    def answer(i):
+        value = total(i)
+        rz[i].wait_recv()
+        value = value + z_in[i].astype(F32)
+        reply[i] = (affinity[:, :1] * value).astype(BF16)
+        for step in (1, 2, 3):
+            bx.append(
+                send(
+                    reply.at[i, sixteen((t + step) % NX)], returned.at[i, sixteen(t)],
+                    bx_send.at[i, step - 1], bx_recv.at[i, step - 1], at_x(step),
+                )
+            )
+        returned[i, sixteen(t), :] = reply[i, sixteen(t), :]
+
+    last = []
+
+    def finish(i):
+        for copy in bx[3 * i : 3 * i + 3]:
+            copy.wait_recv()
+        cols = pl.ds(i * WIDE, WIDE)
+        placed = jnp.dot(onehot[...], returned[i], preferred_element_type=F32)
+        layer[i] = (hidden[:, cols].astype(F32) + placed.astype(BF16).astype(F32)).astype(BF16)
+        last.append(
+            send(layer.at[i], out.at[:, cols], hp_send.at[i], hp_recv.at[i], ((p + 1) % NP, e, t))
+        )
+
     back(0, 0)
     back(1, 0)
-    expert(1, 0)
-    for flow in (2, 3):
-        pass_on(flow, 3)
+    down(0, 0)
     back(0, 1)
     back(1, 1)
     for flow in (2, 3):
         for copy in flying[flow]:
             copy.wait_recv()
-    expert(1, 4)
-    rz = []
-    for flow, hop in ((2, 0), (3, 0), (0, 2), (2, 1), (3, 1), (2, 2), (3, 2), (2, 3), (3, 3)):
+    up(1, 4)
+    down(1, 4)
+    back(2, 0)
+    back(3, 0)
+    down(1, 0)
+    for flow, hop in ((2, 1), (3, 1), (2, 2), (3, 2), (2, 3), (3, 3), (0, 2), (1, 2)):
         back(flow, hop)
-    back(1, 2)
-
-    def home(i):
-        z_out[i] = total(2 + i).astype(BF16)
-        rz.append(send(z_out.at[i], z_in.at[i], rz_send.at[i], rz_recv.at[i], at_z(2)))
-
     home(0)
     back(0, 3)
     home(1)
     back(1, 3)
-    for i in range(2):
-        value = total(i)
-        rz[i].wait_recv()
-        value = value + z_in[i].astype(F32)
-        rows = pl.ds(i * 32, 32)
-        reply[rows, :] = (affinity[rows, :1] * value).astype(BF16)
-
-    bx = []
-    for step in (1, 2, 3):
-        bx.append(
-            send(
-                reply.at[sixteen((t + step) % NX)], returned.at[sixteen(t)],
-                bx_send.at[step - 1], bx_recv.at[step - 1], at_x(step),
-            )
-        )
-    returned[sixteen(t), :] = reply[sixteen(t), :]
-    for copy in bx:
+    answer(0)
+    finish(0)
+    answer(1)
+    finish(1)
+    for copy in last:
         copy.wait_recv()
-    for c in range(4):
-        cols = pl.ds(c * 512, 512)
-        placed = jnp.dot(onehot[...], returned[:, cols], preferred_element_type=F32)
-        layer[:, cols] = (
-            hidden[:, cols].astype(F32) + placed.astype(BF16).astype(F32)
-        ).astype(BF16)
-    last = send(layer, out, hp_send, hp_recv, ((p + 1) % NP, e, t))
-    last.wait_recv()
     for copy in pending:
         copy.wait_send()
 
 
 def shards(context, attn_weight, residual, norm_gain, centroid, w_in, w_out, route_order):
-    vmem, hbm = pl.BlockSpec(memory_space=pltpu.VMEM), pl.BlockSpec(memory_space=pl.ANY)
+    hbm = pl.BlockSpec(memory_space=pl.ANY)
     dma = pltpu.SemaphoreType.DMA
     flows = (4, HOPS, 2)
     result = pl.pallas_call(
         body,
         out_shape=jax.ShapeDtypeStruct((ROWS, D), BF16),
-        in_specs=[vmem, vmem, vmem, vmem, vmem, hbm, hbm, vmem],
+        in_specs=[hbm] * 8,
         out_specs=hbm,
         scratch_shapes=[
+            pltpu.VMEM((4 * ROWS, HEADS), BF16),
+            pltpu.VMEM((ROWS, D), BF16),
+            pltpu.VMEM((1, D), F32),
+            pltpu.VMEM((1, D), BF16),
+            pltpu.VMEM((1, ROWS), jnp.int32),
             pltpu.VMEM((NY, 4 * ROWS, HEADS), BF16),
             pltpu.VMEM((NY, 4 * ROWS, 256), BF16),
             pltpu.VMEM((3, NY, ROWS, 256), BF16),
@@ -374,18 +402,18 @@
             pltpu.VMEM((2, NY, ROWS, D), BF16),
             pltpu.VMEM((D, 2 * UNITS), BF16),
             pltpu.VMEM((2 * UNITS, D), BF16),
-            pltpu.VMEM((4 * ROWS, 2 * UNITS), BF16),
+            pltpu.VMEM((2, NY * ROWS, 2 * UNITS), BF16),
             pltpu.VMEM((2, NY * ROWS, D), F32),
-            pltpu.VMEM((4, HOPS, 2, 32, D), BF16),
-            pltpu.VMEM((4, HOPS, 2, 32, D), BF16),
-            pltpu.VMEM((2, 32, D), BF16),
-            pltpu.VMEM((2, 32, D), BF16),
-            pltpu.VMEM((ROWS, D), BF16),
-            pltpu.VMEM((ROWS, D), BF16),
-            pltpu.VMEM((ROWS, D), BF16),
+            pltpu.VMEM((4, HOPS, 2, ROWS, WIDE), BF16),
+            pltpu.VMEM((4, HOPS, 2, ROWS, WIDE), BF16),
+            pltpu.VMEM((2, ROWS, WIDE), BF16),
+            pltpu.VMEM((2, ROWS, WIDE), BF16),
+            pltpu.VMEM((2, ROWS, WIDE), BF16),
+            pltpu.VMEM((2, ROWS, WIDE), BF16),
+            pltpu.VMEM((2, ROWS, WIDE), BF16),
             pltpu.VMEM((ROWS, 128), F32),
             pltpu.VMEM((ROWS, ROWS), BF16),
-            dma((2,)),
+            dma((8,)),
             dma((4,)), dma((4,)),
             dma((3,)), dma((3,)),
             dma(flows), dma(flows),
@@ -395,17 +423,17 @@
             dma(flows), dma(flows),
             dma(flows), dma(flows),
             dma((2,)), dma((2,)),
-            dma((3,)), dma((3,)),
-            dma, dma,
+            dma((2, 3)), dma((2, 3)),
+            dma((2,)), dma((2,)),
         ],
         compiler_params=pltpu.CompilerParams(
-            collective_id=0, has_side_effects=True, vmem_limit_bytes=48 * 2**20
+            collective_id=0, has_side_effects=True, vmem_limit_bytes=60 * 2**20
         ),
         cost_estimate=pl.CostEstimate(
             flops=4_800_000_000, bytes_accessed=4_000_000, transcendentals=600_000
         ),
     )(
-        context[0], attn_weight[0], residual[0], norm_gain, centroid[0],
+        context[0], attn_weight[0].T, residual[0], norm_gain, centroid[0],
         w_in[0, 0], w_out[0, 0], route_order[0],
     )
     return result[None]

time: 174 us -> 148 us (0.85)
  the two profiles are of different devices: /device:TPU:81 before, /device:TPU:1 now
where the time goes in v2:
time: 148 us; the launch traced here: 147 us
  Pallas kernels  146 us (99%)
  local copies, waits for them, and re-layouts  1.67 us (1%)
    pallas_call x1, Pallas kernels, shards(): pl.pallas_call(body, out_shape=jax.ShapeDtypeStruct((ROWS, D), BF16), in_...  146 us

profile of v2, /device:TPU:1, one launch (start us, length us, event | category | flops | bytes accessed | tf_op | source)
XLA Modules:
  0.0 147.5 jit_solution(6897105396573277844)
XLA Ops:
  0.0 145.8 %shard_map.82 = bf16[64,2048]{1,0:T(8,128)(2,1)} custom-call(bf16[256,512]{1,0:T(8,128)(2,1)} %bitcast.13, bf16[64,512]{1,0:T(8,128)(2,1)} %bitcast.15, bf16[64,2048]{1,0:T(8,128)(2,1)} %bitcast.14, f32[1,2048]{1,0:T(1,128)} %gain_hbm.1, bf16[1,2048]{1,0:T(2,128)(2,1)} %bitcast.16, bf16[2048,256]{1,0:T(8,128)(2,1)} %bitcast.11, bf16[256,2048]{1,0:T(8,128)(2,1)} %bitcast.12, ...), custom_call_target="tpu_custom_call" | custom-call | flops 4800000000 | bytes 4000000 | tf_op jit(solution)/shard_map/pallas_call | solution.py:386
  145.8 1.7 %copy.10 = bf16[1,64,2048]{2,1,0:T(8,128)(2,1)} copy(bf16[1,64,2048]{2,1,0:T(8,128)(2,1)} %bitcast.10) | data formatting | bytes 524288

commit v3 on v2

--- a/solution.py
+++ b/solution.py
@@ -16,6 +16,7 @@
 SLOT = {0: 0, 1: 1, -1: 2, 2: 3, -2: 4, 3: 5, -3: 6, 4: 7, -4: 7}
 HOPS = 4
 DIRS = ((0, 1), (1, -1))
+GROUPS = ((0, 5), (5, 3))
 X_BATCHES = ((0, 3), (3, 2), (5, 2), (7, 1))
 
 
@@ -26,7 +27,7 @@
 
 def body(
     ctx_hbm, attn_hbm, res_hbm, gain_hbm, cent_hbm, w_in, w_out, order_hbm, out,
-    ctx, res, gain, cent, order, proj, part, from_x, hidden, outgoing, tokens, w1, w2, act, sums,
+    ctx, res, gain, cent, order, proj, part, from_x, hidden, outgoing, raw, tokens, w1, w2, act, sums,
     rs_out, rs_in, z_out, z_in, reply, returned, layer, affinity, onehot,
     local_sem, wz_send, wz_recv, pz_send, pz_recv, py_send, py_recv, ax_send, ax_recv,
     dx_send, dx_recv, tz_send, tz_recv, ty_send, ty_recv, ry_send, ry_recv,
@@ -101,14 +102,23 @@
 
     flying = [ring(proj_view, 0, 0, py_send, py_recv)]
 
+    def pass_columns(flow, hop):
+        for copy in flying[flow]:
+            copy.wait_recv()
+        flying[flow] = ring(proj_view, flow, hop, py_send, py_recv)
+
+    pass_columns(0, 1)
+
     for flow in (1, 2, 3):
         pz[flow - 1].wait_recv()
         flying.append(ring(proj_view, flow, 0, py_send, py_recv))
+        if flow == 2:
+            pass_columns(0, 2)
 
     half = UNITS // 2
 
-    def units(i):
-        return pl.ds(i * half, half), pl.ds(UNITS + i * half, half)
+    def units(i, start=0, count=half):
+        return pl.ds(i * half + start, count), pl.ds(UNITS + i * half + start, count)
 
     wz_in = []
     for i, step in DIRS:
@@ -116,6 +126,16 @@
         wz_in.append(
             send(w_in.at[:, mine], w1.at[:, there], wz_send.at[i], wz_recv.at[i], at_z(step))
         )
+
+    wz_out = []
+
+    def send_w_out(piece, start, count):
+        for i, step in DIRS:
+            mine, there = units(i, start, count)
+            k = 2 + 2 * piece + i
+            wz_out.append(
+                send(w_out.at[mine], w2.at[there], wz_send.at[k], wz_recv.at[k], at_z(step))
+            )
 
     def project(slot):
         value = lax.dot_general(
@@ -144,71 +164,95 @@
     onehot[...] = (lax.broadcasted_iota(jnp.int32, (ROWS, ROWS), 0) == order[...]).astype(BF16)
     shared = []
     for hop in range(1, HOPS):
-        for flow in range(4):
-            for copy in flying[flow]:
-                copy.wait_recv()
-            flying[flow] = ring(proj_view, flow, hop, py_send, py_recv)
+        for flow in (1, 2, 3):
+            pass_columns(flow, hop)
+            if (flow, hop) == (2, 1):
+                pass_columns(0, 3)
         project(2 * hop - 1)
         project(2 * hop)
         shared.append(share(hop - 1))
+
+    def sixteen(k):
+        return pl.ds(pl.multiple_of(k * 16, 16), 16)
+
+    def block_columns(offset):
+        return pl.ds(pl.multiple_of((y + offset + 2 * NY) % NY * 256, 256), 256)
+
+    dx = []
+
+    def dispatch(group, batches):
+        first, count = GROUPS[group]
+        for batch in batches:
+            for copy in shared[batch]:
+                copy.wait_recv()
+        for slot in range(first, first + count):
+            attended = part[
+                slot, pl.ds(pl.multiple_of(t * ROWS, ROWS), ROWS), :
+            ].astype(F32)
+            for other in range(3):
+                attended = attended + from_x[other, slot].astype(F32)
+            cols = block_columns(OFFSETS[slot])
+            value = (res[:, cols].astype(F32) + attended).astype(BF16)
+            hidden[:, cols] = value
+            picked = lax.dot_general(
+                onehot[...], value, (((0,), (0,)), ((), ())), preferred_element_type=F32
+            )
+            outgoing[slot] = picked.astype(BF16)
+        slots = pl.ds(first, count)
+        for step in (1, 2, 3):
+            dx.append(
+                send(
+                    outgoing.at[slots, sixteen((t + step) % NX)], raw.at[0, 0, slots, sixteen(t)],
+                    dx_send.at[group, step - 1], dx_recv.at[group, step - 1], at_x(step),
+                )
+            )
+        for slot in range(first, first + count):
+            raw[0, 0, slot, sixteen(t), :] = outgoing[slot, sixteen(t), :]
+
+    def token_view(flow, slot, half):
+        slots = pl.ds(*GROUPS[flow % 2])
+        if half is None:
+            return raw.at[flow // 2, slot, slots]
+        return raw.at[flow // 2, slot, slots, pl.ds(half * 32, 32)]
+
+    tz = []
+
+    def depart(group):
+        for copy in dx[3 * group : 3 * group + 3]:
+            copy.wait_recv()
+        flying_tokens.append(ring(token_view, group, 0, ty_send, ty_recv))
+        tz.append(
+            send(
+                token_view(group, 0, None), token_view(2 + group, 0, None),
+                tz_send.at[group], tz_recv.at[group], at_z(2),
+            )
+        )
+
+    flying_tokens = []
+    dispatch(0, (0, 1))
     for flow in range(4):
         for copy in flying[flow]:
             copy.wait_recv()
     project(7)
     shared.append(share(3))
-
-    squares = jnp.zeros((ROWS, 1), F32)
-    for batch, (first, count) in enumerate(X_BATCHES):
-        for copy in shared[batch]:
-            copy.wait_recv()
-        for slot in range(first, first + count):
-            mine = part[slot, pl.ds(pl.multiple_of(t * ROWS, ROWS), ROWS), :].astype(F32)
-            attended = mine
-            for other in range(3):
-                attended = attended + from_x[other, slot].astype(F32)
-            cols = pl.ds(pl.multiple_of((y + OFFSETS[slot] + NY) % NY * 256, 256), 256)
-            value = (res[:, cols].astype(F32) + attended).astype(BF16)
-            hidden[:, cols] = value
-            wide = value.astype(F32)
-            squares = squares + jnp.sum(wide * wide, axis=-1, keepdims=True)
-    inverse_rms = lax.rsqrt(squares * (1.0 / D) + 1e-05)
-    for c in range(4):
-        cols = pl.ds(c * 512, 512)
-        normed = (hidden[:, cols].astype(F32) * inverse_rms * gain[:, cols]).astype(BF16)
-        picked = lax.dot_general(
-            onehot[...], normed, (((0,), (0,)), ((), ())), preferred_element_type=F32
-        )
-        outgoing[:, cols] = picked.astype(BF16)
-
-    def sixteen(k):
-        return pl.ds(pl.multiple_of(k * 16, 16), 16)
-
-    dx = []
-    for step in (1, 2, 3):
-        dx.append(
-            send(
-                outgoing.at[sixteen((t + step) % NX)], tokens.at[0, 0, sixteen(t)],
-                dx_send.at[step - 1], dx_recv.at[step - 1], at_x(step),
-            )
-        )
-    tokens[0, 0, sixteen(t), :] = outgoing[sixteen(t), :]
-    for copy in dx:
-        copy.wait_recv()
-
-    def token_view(flow, slot, quarter):
-        start, count = flow % 2 * 32, 32
-        if quarter is not None:
-            start, count = start + quarter * 16, 16
-        return tokens.at[flow // 2, slot, pl.ds(start, count)]
-
-    flying = [ring(token_view, flow, 0, ty_send, ty_recv) for flow in (0, 1)]
-    tz = []
-    for i in range(2):
-        rows = pl.ds(i * 32, 32)
-        tz.append(
-            send(tokens.at[0, 0, rows], tokens.at[1, 0, rows], tz_send.at[i], tz_recv.at[i], at_z(2))
-        )
-
+    depart(0)
+    dispatch(1, (2, 3))
+    depart(1)
+    flying = flying_tokens
+
+    def norm(source, slots):
+        for slot in slots:
+            squares = jnp.zeros((ROWS, 1), F32)
+            for q in range(NY):
+                value = raw[source, slot, q].astype(F32)
+                squares = squares + jnp.sum(value * value, axis=-1, keepdims=True)
+            inverse_rms = lax.rsqrt(squares * (1.0 / D) + 1e-05)
+            for q in range(NY):
+                cols = block_columns(OFFSETS[slot] + OFFSETS[q])
+                value = raw[source, slot, q].astype(F32) * inverse_rms * gain[:, cols]
+                tokens[source, slot, :, cols] = value.astype(BF16)
+
+    norm(0, (0,))
     dots = jnp.zeros((ROWS, 1), F32)
     for c in range(4):
         cols = pl.ds(c * 512, 512)
@@ -246,31 +290,32 @@
 
         lax.fori_loop(0, 4, tile, 0)
 
-    for hop in range(1, HOPS):
+    for hop in (1, 2):
         for flow in (0, 1):
             pass_on(flow, hop)
-    for i in range(2):
-        tz[i].wait_recv()
-        flying.append(ring(token_view, 2 + i, 0, ty_send, ty_recv))
-    wz_out = []
-    for i, step in DIRS:
-        mine, there = units(i)
-        wz_out.append(
-            send(w_out.at[mine], w2.at[there], wz_send.at[2 + i], wz_recv.at[2 + i], at_z(step))
-        )
+    tz[0].wait_recv()
+    flying.append(ring(token_view, 2, 0, ty_send, ty_recv))
+    for flow in (0, 1):
+        pass_on(flow, 3)
+    tz[1].wait_recv()
+    flying.append(ring(token_view, 3, 0, ty_send, ty_recv))
+    send_w_out(0, 0, half)
     for copy in loads[6:]:
         copy.wait()
     for copy in wz_in:
         copy.wait_recv()
+    norm(0, (1, 2, 3))
     up(0, 0)
     for flow in (2, 3):
         pass_on(flow, 1)
     for flow in (0, 1):
         for copy in flying[flow]:
             copy.wait_recv()
+    norm(0, (4, 5, 6, 7))
     up(0, 4)
     for flow in (2, 3):
         pass_on(flow, 2)
+    norm(1, (0, 1, 2, 3))
     up(1, 0)
     for flow in (2, 3):
         pass_on(flow, 3)
@@ -358,20 +403,21 @@
     for flow in (2, 3):
         for copy in flying[flow]:
             copy.wait_recv()
+    norm(1, (4, 5, 6, 7))
     up(1, 4)
     down(1, 4)
     back(2, 0)
     back(3, 0)
     down(1, 0)
-    for flow, hop in ((2, 1), (3, 1), (2, 2), (3, 2), (2, 3), (3, 3), (0, 2), (1, 2)):
+    for flow, hop in ((2, 1), (3, 1), (2, 2), (3, 2), (2, 3), (0, 2), (3, 3), (1, 2)):
         back(flow, hop)
     home(0)
     back(0, 3)
     home(1)
     back(1, 3)
     answer(0)
+    answer(1)
     finish(0)
-    answer(1)
     finish(1)
     for copy in last:
         copy.wait_recv()
@@ -398,7 +444,8 @@
             pltpu.VMEM((NY, 4 * ROWS, 256), BF16),
             pltpu.VMEM((3, NY, ROWS, 256), BF16),
             pltpu.VMEM((ROWS, D), BF16),
-            pltpu.VMEM((ROWS, D), BF16),
+            pltpu.VMEM((NY, ROWS, 256), BF16),
+            pltpu.VMEM((2, NY, NY, ROWS, 256), BF16),
             pltpu.VMEM((2, NY, ROWS, D), BF16),
             pltpu.VMEM((D, 2 * UNITS), BF16),
             pltpu.VMEM((2 * UNITS, D), BF16),
@@ -418,7 +465,7 @@
             dma((3,)), dma((3,)),
             dma(flows), dma(flows),
             dma((4, 3)), dma((4, 3)),
-            dma((3,)), dma((3,)),
+            dma((2, 3)), dma((2, 3)),
             dma((2,)), dma((2,)),
             dma(flows), dma(flows),
             dma(flows), dma(flows),

time: 148 us -> 142 us (0.959)
  Pallas kernels: 146 us -> 140 us
    pallas_call x1, Pallas kernels: 146 us -> 140 us  [shards(): pl.pallas_call(body, out_shape=jax.ShapeDtypeStruct((ROWS, D), BF16), in_...]
where the time goes in v3:
time: 142 us
  Pallas kernels  140 us (99%)
  local copies, waits for them, and re-layouts  1.67 us (1%)
    pallas_call x1, Pallas kernels, shards(): pl.pallas_call(body, out_shape=jax.ShapeDtypeStruct((ROWS, D), BF16), in_...  140 us

profile of v3, /device:TPU:1, one launch (start us, length us, event | category | flops | bytes accessed | tf_op | source)
XLA Modules:
  0.0 142.0 jit_solution(14925951653425342634)
XLA Ops:
  0.0 140.3 %shard_map.82 = bf16[64,2048]{1,0:T(8,128)(2,1)} custom-call(bf16[256,512]{1,0:T(8,128)(2,1)} %bitcast.13, bf16[64,512]{1,0:T(8,128)(2,1)} %bitcast.15, bf16[64,2048]{1,0:T(8,128)(2,1)} %bitcast.14, f32[1,2048]{1,0:T(1,128)} %gain_hbm.1, bf16[1,2048]{1,0:T(2,128)(2,1)} %bitcast.16, bf16[2048,256]{1,0:T(8,128)(2,1)} %bitcast.11, bf16[256,2048]{1,0:T(8,128)(2,1)} %bitcast.12, ...), custom_call_target="tpu_custom_call" | custom-call | flops 4800000000 | bytes 4000000 | tf_op jit(solution)/shard_map/pallas_call | solution.py:432
  140.3 1.7 %copy.10 = bf16[1,64,2048]{2,1,0:T(8,128)(2,1)} copy(bf16[1,64,2048]{2,1,0:T(8,128)(2,1)} %bitcast.10) | data formatting | bytes 524288

commit v4 on v3

--- a/solution.py
+++ b/solution.py
@@ -295,11 +295,11 @@
             pass_on(flow, hop)
     tz[0].wait_recv()
     flying.append(ring(token_view, 2, 0, ty_send, ty_recv))
-    for flow in (0, 1):
-        pass_on(flow, 3)
+    pass_on(0, 3)
     tz[1].wait_recv()
     flying.append(ring(token_view, 3, 0, ty_send, ty_recv))
     send_w_out(0, 0, half)
+    pass_on(1, 3)
     for copy in loads[6:]:
         copy.wait()
     for copy in wz_in:

time: 142 us -> 142 us (level)
  no operation moved by 1% of the time
where the time goes in v4:
time: 142 us
  Pallas kernels  140 us (99%)
  local copies, waits for them, and re-layouts  1.67 us (1%)
    pallas_call x1, Pallas kernels, shards(): pl.pallas_call(body, out_shape=jax.ShapeDtypeStruct((ROWS, D), BF16), in_...  140 us

profile of v4, /device:TPU:1, one launch (start us, length us, event | category | flops | bytes accessed | tf_op | source)
XLA Modules:
  0.0 141.9 jit_solution(8851760834160566077)
XLA Ops:
  0.0 140.3 %shard_map.82 = bf16[64,2048]{1,0:T(8,128)(2,1)} custom-call(bf16[256,512]{1,0:T(8,128)(2,1)} %bitcast.13, bf16[64,512]{1,0:T(8,128)(2,1)} %bitcast.15, bf16[64,2048]{1,0:T(8,128)(2,1)} %bitcast.14, f32[1,2048]{1,0:T(1,128)} %gain_hbm.1, bf16[1,2048]{1,0:T(2,128)(2,1)} %bitcast.16, bf16[2048,256]{1,0:T(8,128)(2,1)} %bitcast.11, bf16[256,2048]{1,0:T(8,128)(2,1)} %bitcast.12, ...), custom_call_target="tpu_custom_call" | custom-call | flops 4800000000 | bytes 4000000 | tf_op jit(solution)/shard_map/pallas_call | solution.py:432
  140.3 1.7 %copy.10 = bf16[1,64,2048]{2,1,0:T(8,128)(2,1)} copy(bf16[1,64,2048]{2,1,0:T(8,128)(2,1)} %bitcast.10) | data formatting | bytes 524288
